TPU v7x, 768 devices: a whole 4x8x12 slice. The times are simulated.
768 devices in a mesh: ctx: 12 (over z), tp: 8 (over x, core), grp: 8 (over y).
Axes of the slice: x: 4, y: 8, z: 12, core: 2. Of those that a mesh axis runs over, the one named last changes fastest.
Arguments:
- queries: bfloat16 [24576, 8192], P(('ctx', 'grp'), 'tp'), may hold values from -24 to 24
- keys: bfloat16 [24576, 1024], P(('ctx', 'grp'), 'tp'), may hold values from -4 to 4
- values: bfloat16 [24576, 1024], P(('ctx', 'grp'), 'tp'), may hold values from -6 to 6
- output_gradient: bfloat16 [24576, 8192], P(('ctx', 'grp'), 'tp'), may hold values from -6 to 6
- doc_tiles: int32 [32], replicated, may hold values from 1 to 8, 192 in all
- doc_pads: int32 [32], replicated, may hold values from 0 to 127
Outputs:
- grad_queries: bfloat16 [24576, 8192], P(('ctx', 'grp'), 'tp')
- grad_keys: bfloat16 [24576, 1024], P(('ctx', 'grp'), 'tp')
- grad_values: bfloat16 [24576, 1024], P(('ctx', 'grp'), 'tp')
All inputs are finite; a program needn't handle non-finite values.
Results may differ from a plain program's by a relative error of at most 0.0081.
Values may be sent and summed in bfloat16 or wider, within the bound.
A program may use at most 64 MiB of HBM per device.

v0:
```python
import jax
import jax.numpy as jnp
from jax import lax
from jax.sharding import PartitionSpec as P

HEAD_SIZE = 128
TILE = 128
REACH = 4


def passed_along(value, axis, by):
    length = lax.axis_size(axis)
    pairs = [(i, i + by) for i in range(length) if 0 <= i + by < length]
    return lax.ppermute(value, axis, pairs)


def token_table(doc_tiles, doc_pads, index):
    count = doc_tiles.shape[0]
    starts = (jnp.cumsum(doc_tiles, dtype=jnp.int32) - doc_tiles) * TILE
    ends = starts + doc_tiles * TILE - doc_pads
    found = (starts[None, :] <= index[:, None]).astype(jnp.int32)
    doc = jnp.sum(found, axis=1, dtype=jnp.int32) - 1
    match = (doc[:, None] == jnp.arange(count, dtype=jnp.int32)[None, :]).astype(jnp.int32)
    end_of = jnp.sum(match * ends[None, :], axis=1, dtype=jnp.int32)
    live = (doc >= 0) & (index < end_of)
    return (doc, live)


def attend(qh, kh, vh, gh, qidx, kidx, qdoc, qok, kdoc, kok):
    scale = 1.0 / jnp.sqrt(jnp.float32(qh.shape[-1]))
    allowed = (
        (qdoc[:, None] == kdoc[None, :])
        & qok[:, None]
        & kok[None, :]
        & (kidx[None, :] <= qidx[:, None])
    )
    scores = jnp.einsum("qgd,kd->gqk", qh, kh, preferred_element_type=jnp.float32) * scale
    masked = jnp.where(allowed[None], scores, jnp.float32(-1e30))
    top = jnp.max(masked, axis=-1, keepdims=True)
    weights = jnp.where(allowed[None], jnp.exp(masked - top), jnp.float32(0.0))
    total = jnp.sum(weights, axis=-1)
    total = jnp.where(qok[None, :], total, jnp.float32(1.0))
    probs = (weights / total[..., None]).astype(jnp.bfloat16)
    out = jnp.einsum("gqk,kd->qgd", probs, vh, preferred_element_type=jnp.float32)
    delta = jnp.sum(gh.astype(jnp.float32) * out, axis=-1)
    dprob = jnp.einsum("qgd,kd->gqk", gh, vh, preferred_element_type=jnp.float32)
    dscore = (probs.astype(jnp.float32) * (dprob - jnp.transpose(delta)[..., None])).astype(
        jnp.bfloat16
    )
    grad_q = jnp.einsum("gqk,kd->qgd", dscore, kh, preferred_element_type=jnp.float32) * scale
    key_gradient = jnp.einsum("gqk,qgd->kd", dscore, qh, preferred_element_type=jnp.float32) * scale
    value_gradient = jnp.einsum("gqk,qgd->kd", probs, gh, preferred_element_type=jnp.float32)
    return (grad_q, key_gradient, value_gradient)


def shards(queries, keys, values, output_gradient, doc_tiles, doc_pads):
    rows = queries.shape[0]
    local_kv = keys.shape[1] // HEAD_SIZE
    head_group = queries.shape[1] // keys.shape[1]
    heads = local_kv * head_group
    mine = lax.axis_index(("ctx", "grp"))
    before = [
        passed_along((keys, values), ("ctx", "grp"), distance) for distance in range(REACH, 0, -1)
    ]
    key_rows = jnp.concatenate([piece[0] for piece in before] + [keys], axis=0)
    value_rows = jnp.concatenate([piece[1] for piece in before] + [values], axis=0)
    window_width = key_rows.shape[0]
    qidx = mine * rows + jnp.arange(rows, dtype=jnp.int32)
    kidx = (mine - REACH) * rows + jnp.arange(window_width, dtype=jnp.int32)
    qdoc, qok = token_table(doc_tiles, doc_pads, qidx)
    kdoc, kok = token_table(doc_tiles, doc_pads, kidx)
    q_heads = jnp.transpose(queries.reshape(rows, heads, HEAD_SIZE), (1, 0, 2))
    g_heads = jnp.transpose(output_gradient.reshape(rows, heads, HEAD_SIZE), (1, 0, 2))
    k_heads = jnp.repeat(
        jnp.transpose(key_rows.reshape(window_width, local_kv, HEAD_SIZE), (1, 0, 2)),
        head_group,
        axis=0,
    )
    v_heads = jnp.repeat(
        jnp.transpose(value_rows.reshape(window_width, local_kv, HEAD_SIZE), (1, 0, 2)),
        head_group,
        axis=0,
    )
    first = (REACH - REACH) * rows

    def head(pieces):
        qh, kh, vh, gh = pieces
        grad_q, key_gradient, value_gradient = attend(
            qh[:, None, :], kh, vh, gh[:, None, :], qidx, kidx, qdoc, qok, kdoc, kok
        )
        return (grad_q[:, 0, :], key_gradient, value_gradient)

    grad_q, key_gradient, value_gradient = lax.map(head, (q_heads, k_heads, v_heads, g_heads))
    key_gradient = jnp.sum(
        key_gradient.reshape(local_kv, head_group, window_width - first, HEAD_SIZE), axis=1
    )
    value_gradient = jnp.sum(
        value_gradient.reshape(local_kv, head_group, window_width - first, HEAD_SIZE), axis=1
    )
    padding = jnp.zeros((local_kv, first, HEAD_SIZE), jnp.float32)
    key_gradient = jnp.concatenate([padding, key_gradient], axis=1)
    value_gradient = jnp.concatenate([padding, value_gradient], axis=1)
    grad_q, key_gradient, value_gradient = (grad_q, key_gradient, value_gradient)
    grad_queries = (
        jnp.transpose(grad_q, (1, 0, 2)).reshape(rows, queries.shape[1]).astype(jnp.bfloat16)
    )
    key_grads = jnp.transpose(key_gradient, (1, 0, 2)).reshape(window_width, keys.shape[1])
    value_grads = jnp.transpose(value_gradient, (1, 0, 2)).reshape(window_width, keys.shape[1])

    def portion(distance):
        first = (REACH - distance) * rows
        return (key_grads[first : first + rows], value_grads[first : first + rows])

    own_k, own_v = portion(0)
    for distance in range(1, REACH + 1):
        came_k, came_v = passed_along(portion(distance), ("ctx", "grp"), -distance)
        own_k = own_k + came_k
        own_v = own_v + came_v
    return (grad_queries, own_k.astype(jnp.bfloat16), own_v.astype(jnp.bfloat16))


def solution(mesh):
    in_specs = (
        P(("ctx", "grp"), "tp"),
        P(("ctx", "grp"), "tp"),
        P(("ctx", "grp"), "tp"),
        P(("ctx", "grp"), "tp"),
        P(),
        P(),
    )
    out_specs = (P(("ctx", "grp"), "tp"), P(("ctx", "grp"), "tp"), P(("ctx", "grp"), "tp"))
    return jax.shard_map(shards, mesh=mesh, in_specs=in_specs, out_specs=out_specs, check_vma=False)
```

profile of v0, /device:TPU:197, one launch (start us, length us, event | category | flops | bytes accessed | tf_op | source)
XLA Modules:
  0.0 214.5 jit_solution(1359585853187218736)
XLA Ops:
  0.7 4.4 %collective-permute-start.2 = (bf16[256,128]{1,0:T(8,128)(2,1)}, bf16[256,128]{1,0:T(8,128)(2,1)S(1)}, u32[]{:S(2)}, u32[]{:S(2)}) collective-permute-start(bf16[256,128]{1,0:T(8,128)(2,1)} %param.9), channel_id=1, source_target_pairs={{0,2},{1,3},{2,4},{3,5},{4,6},{5,7},{6,64},{7,65},{64,66},{65,67},... | collective-permute-start | bytes 196616 | tf_op jit(solution)/shard_map/ppermute | solution.py:14
  5.0 5.5 %collective-permute-start.1 = (bf16[256,128]{1,0:T(8,128)(2,1)}, bf16[256,128]{1,0:T(8,128)(2,1)S(1)}, u32[]{:S(2)}, u32[]{:S(2)}) collective-permute-start(bf16[256,128]{1,0:T(8,128)(2,1)} %param.9), channel_id=1, source_target_pairs={{0,3},{1,4},{2,5},{3,6},{4,7},{5,64},{6,65},{7,66},{64,67},{65,68}... | collective-permute-start | bytes 196616 | tf_op jit(solution)/shard_map/ppermute | solution.py:14
  10.6 5.7 %collective-permute-start = (bf16[256,128]{1,0:T(8,128)(2,1)}, bf16[256,128]{1,0:T(8,128)(2,1)S(1)}, u32[]{:S(2)}, u32[]{:S(2)}) collective-permute-start(bf16[256,128]{1,0:T(8,128)(2,1)} %param.9), channel_id=1, source_target_pairs={{0,4},{1,5},{2,6},{3,7},{4,64},{5,65},{6,66},{7,67},{64,68},{65,69... | collective-permute-start | bytes 196616 | tf_op jit(solution)/shard_map/ppermute | solution.py:14
  16.2 3.2 %collective-permute-start.3 = (bf16[256,128]{1,0:T(8,128)(2,1)}, bf16[256,128]{1,0:T(8,128)(2,1)S(1)}, u32[]{:S(2)}, u32[]{:S(2)}) collective-permute-start(bf16[256,128]{1,0:T(8,128)(2,1)} %param.9), channel_id=1, source_target_pairs={{0,1},{1,2},{2,3},{3,4},{4,5},{5,6},{6,7},{7,64},{64,65},{65,66},{... | collective-permute-start | bytes 196616 | tf_op jit(solution)/shard_map/ppermute | solution.py:14
  19.4 5.7 %collective-permute-start.4 = (bf16[256,128]{1,0:T(8,128)(2,1)}, bf16[256,128]{1,0:T(8,128)(2,1)S(1)}, u32[]{:S(2)}, u32[]{:S(2)}) collective-permute-start(bf16[256,128]{1,0:T(8,128)(2,1)} %param.10), channel_id=1, source_target_pairs={{0,4},{1,5},{2,6},{3,7},{4,64},{5,65},{6,66},{7,67},{64,68},{65,69... | collective-permute-start | bytes 196616 | tf_op jit(solution)/shard_map/ppermute | solution.py:14
  27.2 2.1 copy.18
  29.5 6.1 %collective-permute-start.5 = (bf16[256,128]{1,0:T(8,128)(2,1)S(1)}, bf16[256,128]{1,0:T(8,128)(2,1)S(1)}, u32[]{:S(2)}, u32[]{:S(2)}) collective-permute-start(bf16[256,128]{1,0:T(8,128)(2,1)S(1)} %copy-done.2), channel_id=1, source_target_pairs={{0,3},{1,4},{2,5},{3,6},{4,7},{5,64},{6,65},{7,66},{64,67},{65,68}... | collective-permute-start | bytes 196616 | tf_op jit(solution)/shard_map/ppermute | solution.py:14
  35.6 3.4 %collective-permute-done.5 = bf16[256,128]{1,0:T(8,128)(2,1)S(1)} collective-permute-done((bf16[256,128]{1,0:T(8,128)(2,1)S(1)}, bf16[256,128]{1,0:T(8,128)(2,1)S(1)}, u32[]{:S(2)}, u32[]{:S(2)}) %collective-permute-start.5) | collective-permute-done | bytes 65568 | tf_op jit(solution)/shard_map/ppermute | solution.py:14
  39.1 4.7 %collective-permute-start.6 = (bf16[256,128]{1,0:T(8,128)(2,1)S(1)}, bf16[256,128]{1,0:T(8,128)(2,1)S(1)}, u32[]{:S(2)}, u32[]{:S(2)}) collective-permute-start(bf16[256,128]{1,0:T(8,128)(2,1)S(1)} %copy-done.2), channel_id=1, source_target_pairs={{0,2},{1,3},{2,4},{3,5},{4,6},{5,7},{6,64},{7,65},{64,66},{65,67},... | collective-permute-start | bytes 196616 | tf_op jit(solution)/shard_map/ppermute | solution.py:14
  43.8 3.9 %collective-permute-done.6 = bf16[256,128]{1,0:T(8,128)(2,1)S(1)} collective-permute-done((bf16[256,128]{1,0:T(8,128)(2,1)S(1)}, bf16[256,128]{1,0:T(8,128)(2,1)S(1)}, u32[]{:S(2)}, u32[]{:S(2)}) %collective-permute-start.6) | collective-permute-done | bytes 65568 | tf_op jit(solution)/shard_map/ppermute | solution.py:14
  47.8 2.9 %collective-permute-start.7 = (bf16[256,128]{1,0:T(8,128)(2,1)S(1)}, bf16[256,128]{1,0:T(8,128)(2,1)S(1)}, u32[]{:S(2)}, u32[]{:S(2)}) collective-permute-start(bf16[256,128]{1,0:T(8,128)(2,1)S(1)} %copy-done.2), channel_id=1, source_target_pairs={{0,1},{1,2},{2,3},{3,4},{4,5},{5,6},{6,7},{7,64},{64,65},{65,66},{... | collective-permute-start | bytes 196616 | tf_op jit(solution)/shard_map/ppermute | solution.py:14
  50.7 4.1 %collective-permute-done.7 = bf16[256,128]{1,0:T(8,128)(2,1)S(1)} collective-permute-done((bf16[256,128]{1,0:T(8,128)(2,1)S(1)}, bf16[256,128]{1,0:T(8,128)(2,1)S(1)}, u32[]{:S(2)}, u32[]{:S(2)}) %collective-permute-start.7) | collective-permute-done | bytes 65568 | tf_op jit(solution)/shard_map/ppermute | solution.py:14
  57.3 79.0 %while.15 = (s32[]{:T(128)}, bf16[8,256,128]{1,2,0:T(8,128)(2,1)}, f32[8,1280,128]{2,1,0:T(8,128)}, f32[8,1280,128]{2,1,0:T(8,128)}, bf16[8,1280,128]{2,1,0:T(8,...) while((s32[]{:T(128)}, bf16[8,256,128]{1,2,0:T(8,128)(2,1)}, ...), condition=%wide.region_9.10_spmd.clone, body=%wide.region_5.9_spmd.clone.sunk | while | flops 513115136 | bytes 11663261 | solution.py:93
  57.3 2.0 fusion.83
  62.1 1.9 fusion.87
  64.0 2.0 fusion.88
  67.1 2.0 fusion.83
  71.9 1.9 fusion.87
  73.8 2.0 fusion.88
  77.0 2.0 fusion.83
  81.8 1.9 fusion.87
  83.7 2.0 fusion.88
  86.9 2.0 fusion.83
  91.6 1.9 fusion.87
  93.6 2.0 fusion.88
  96.7 2.0 fusion.83
  101.5 1.9 fusion.87
  103.4 2.0 fusion.88
  106.6 2.0 fusion.83
  113.3 2.0 fusion.88
  116.5 2.0 fusion.83
  121.3 1.9 fusion.87
  123.2 2.0 fusion.88
  126.4 2.0 fusion.83
  131.1 1.9 fusion.87
  133.0 2.0 fusion.88
  136.2 2.8 %reduce_sum.82 = f32[1280,128]{1,0:T(8,128)S(1)} reduce(f32[8,1280,128]{2,1,0:T(8,128)} %get-tuple-element.79, f32[]{:T(128)} %constant.28.clone.1), dimensions={0}, to_apply=%region_11.12 | reduce | flops 1146880 | bytes 5898244 | tf_op jit(solution)/shard_map/reduce_sum | solution.py:97
  139.1 2.9 %reduce_sum.80 = f32[1280,128]{1,0:T(8,128)S(1)} reduce(f32[8,1280,128]{2,1,0:T(8,128)} %get-tuple-element.78, f32[]{:T(128)} %constant.28.clone.1), dimensions={0}, to_apply=%region_10.11 | reduce | flops 1146880 | bytes 5898244 | tf_op jit(solution)/shard_map/reduce_sum | solution.py:94
  143.0 1.9 collective-permute-start.12
  144.9 1.9 collective-permute-start.15
  146.8 5.4 %collective-permute-start.14 = (f32[256,128]{1,0:T(8,128)S(1)}, f32[256,128]{1,0:T(8,128)S(1)}, u32[]{:S(2)}, u32[]{:S(2)}) collective-permute-start(f32[256,128]{1,0:T(8,128)S(1)} %get-tuple-element.173), channel_id=1, source_target_pairs={{3,0},{4,1},{5,2},{6,3},{7,4},{64,5},{65,6},{66,7},{67,64},{68,65}... | collective-permute-start | bytes 393224 | tf_op jit(solution)/shard_map/ppermute | solution.py:14
  152.2 1.9 collective-permute-start.13
  154.2 2.2 %collective-permute-start.8 = (f32[256,128]{1,0:T(8,128)S(1)}, f32[256,128]{1,0:T(8,128)S(1)}, u32[]{:S(2)}, u32[]{:S(2)}) collective-permute-start(f32[256,128]{1,0:T(8,128)S(1)} %get-tuple-element.175), channel_id=1, source_target_pairs={{1,0},{2,1},{3,2},{4,3},{5,4},{6,5},{7,6},{64,7},{65,64},{66,65},{... | collective-permute-start | bytes 393224 | tf_op jit(solution)/shard_map/ppermute | solution.py:14
  156.4 4.8 %collective-permute-start.11 = (f32[256,128]{1,0:T(8,128)S(1)}, f32[256,128]{1,0:T(8,128)S(1)}, u32[]{:S(2)}, u32[]{:S(2)}) collective-permute-start(f32[256,128]{1,0:T(8,128)S(1)} %get-tuple-element.176), channel_id=1, source_target_pairs={{4,0},{5,1},{6,2},{7,3},{64,4},{65,5},{66,6},{67,7},{68,64},{69,65... | collective-permute-start | bytes 393224 | tf_op jit(solution)/shard_map/ppermute | solution.py:14
  161.2 3.4 %collective-permute-start.10 = (f32[256,128]{1,0:T(8,128)S(1)}, f32[256,128]{1,0:T(8,128)S(1)}, u32[]{:S(2)}, u32[]{:S(2)}) collective-permute-start(f32[256,128]{1,0:T(8,128)S(1)} %get-tuple-element.177), channel_id=1, source_target_pairs={{3,0},{4,1},{5,2},{6,3},{7,4},{64,5},{65,6},{66,7},{67,64},{68,65}... | collective-permute-start | bytes 393224 | tf_op jit(solution)/shard_map/ppermute | solution.py:14
  164.7 2.2 %collective-permute-start.9 = (f32[256,128]{1,0:T(8,128)S(1)}, f32[256,128]{1,0:T(8,128)S(1)}, u32[]{:S(2)}, u32[]{:S(2)}) collective-permute-start(f32[256,128]{1,0:T(8,128)S(1)} %get-tuple-element.178), channel_id=1, source_target_pairs={{2,0},{3,1},{4,2},{5,3},{6,4},{7,5},{64,6},{65,7},{66,64},{67,65},... | collective-permute-start | bytes 393224 | tf_op jit(solution)/shard_map/ppermute | solution.py:14
  166.9 39.1 %collective-permute-done.13 = f32[256,128]{1,0:T(8,128)S(1)} collective-permute-done((f32[256,128]{1,0:T(8,128)S(1)}, f32[256,128]{1,0:T(8,128)S(1)}, u32[]{:S(2)}, u32[]{:S(2)}) %collective-permute-start.13) | collective-permute-done | bytes 131104 | tf_op jit(solution)/shard_map/ppermute | solution.py:14
  206.7 7.1 %collective-permute-done.9 = f32[256,128]{1,0:T(8,128)S(1)} collective-permute-done((f32[256,128]{1,0:T(8,128)S(1)}, f32[256,128]{1,0:T(8,128)S(1)}, u32[]{:S(2)}, u32[]{:S(2)}) %collective-permute-start.9) | collective-permute-done | bytes 131104 | tf_op jit(solution)/shard_map/ppermute | solution.py:14
  (119 shorter events, 40.3 us)
Async XLA Ops:
  0.6 28.9 %copy-start.2 = (bf16[256,128]{1,0:T(8,128)(2,1)S(1)}, bf16[256,128]{1,0:T(8,128)(2,1)}, u32[]{:S(2)}) copy-start(bf16[256,128]{1,0:T(8,128)(2,1)} %param.10) | copy-start | bytes 196612
  0.6 28.6 %copy-start = (bf16[256,1024]{1,0:T(8,128)(2,1)S(1)}, bf16[256,1024]{1,0:T(8,128)(2,1)}, u32[]{:S(2)}) copy-start(bf16[256,1024]{1,0:T(8,128)(2,1)} %param.11) | copy-start | bytes 1572868
  0.7 54.3 %collective-permute-start.2 = (bf16[256,128]{1,0:T(8,128)(2,1)}, bf16[256,128]{1,0:T(8,128)(2,1)S(1)}, u32[]{:S(2)}, u32[]{:S(2)}) collective-permute-start(bf16[256,128]{1,0:T(8,128)(2,1)} %param.9), channel_id=1, source_target_pairs={{0,2},{1,3},{2,4},{3,5},{4,6},{5,7},{6,64},{7,65},{64,66},{65,67},... | collective-permute-start | bytes 196616 | tf_op jit(solution)/shard_map/ppermute | solution.py:14
  5.0 49.9 %collective-permute-start.1 = (bf16[256,128]{1,0:T(8,128)(2,1)}, bf16[256,128]{1,0:T(8,128)(2,1)S(1)}, u32[]{:S(2)}, u32[]{:S(2)}) collective-permute-start(bf16[256,128]{1,0:T(8,128)(2,1)} %param.9), channel_id=1, source_target_pairs={{0,3},{1,4},{2,5},{3,6},{4,7},{5,64},{6,65},{7,66},{64,67},{65,68}... | collective-permute-start | bytes 196616 | tf_op jit(solution)/shard_map/ppermute | solution.py:14
  10.6 44.4 %collective-permute-start = (bf16[256,128]{1,0:T(8,128)(2,1)}, bf16[256,128]{1,0:T(8,128)(2,1)S(1)}, u32[]{:S(2)}, u32[]{:S(2)}) collective-permute-start(bf16[256,128]{1,0:T(8,128)(2,1)} %param.9), channel_id=1, source_target_pairs={{0,4},{1,5},{2,6},{3,7},{4,64},{5,65},{6,66},{7,67},{64,68},{65,69... | collective-permute-start | bytes 196616 | tf_op jit(solution)/shard_map/ppermute | solution.py:14
  16.2 38.8 %collective-permute-start.3 = (bf16[256,128]{1,0:T(8,128)(2,1)}, bf16[256,128]{1,0:T(8,128)(2,1)S(1)}, u32[]{:S(2)}, u32[]{:S(2)}) collective-permute-start(bf16[256,128]{1,0:T(8,128)(2,1)} %param.9), channel_id=1, source_target_pairs={{0,1},{1,2},{2,3},{3,4},{4,5},{5,6},{6,7},{7,64},{64,65},{65,66},{... | collective-permute-start | bytes 196616 | tf_op jit(solution)/shard_map/ppermute | solution.py:14
  19.4 10.1 %collective-permute-start.4 = (bf16[256,128]{1,0:T(8,128)(2,1)}, bf16[256,128]{1,0:T(8,128)(2,1)S(1)}, u32[]{:S(2)}, u32[]{:S(2)}) collective-permute-start(bf16[256,128]{1,0:T(8,128)(2,1)} %param.10), channel_id=1, source_target_pairs={{0,4},{1,5},{2,6},{3,7},{4,64},{5,65},{6,66},{7,67},{64,68},{65,69... | collective-permute-start | bytes 196616 | tf_op jit(solution)/shard_map/ppermute | solution.py:14
  29.3 25.8 %copy-start.3 = (bf16[256,128]{1,0:T(8,128)(2,1)S(1)}, bf16[256,128]{1,0:T(8,128)(2,1)}, u32[]{:S(2)}) copy-start(bf16[256,128]{1,0:T(8,128)(2,1)} %param.9) | copy-start | bytes 196612
  29.5 9.6 %collective-permute-start.5 = (bf16[256,128]{1,0:T(8,128)(2,1)S(1)}, bf16[256,128]{1,0:T(8,128)(2,1)S(1)}, u32[]{:S(2)}, u32[]{:S(2)}) collective-permute-start(bf16[256,128]{1,0:T(8,128)(2,1)S(1)} %copy-done.2), channel_id=1, source_target_pairs={{0,3},{1,4},{2,5},{3,6},{4,7},{5,64},{6,65},{7,66},{64,67},{65,68}... | collective-permute-start | bytes 196616 | tf_op jit(solution)/shard_map/ppermute | solution.py:14
  39.1 8.7 %collective-permute-start.6 = (bf16[256,128]{1,0:T(8,128)(2,1)S(1)}, bf16[256,128]{1,0:T(8,128)(2,1)S(1)}, u32[]{:S(2)}, u32[]{:S(2)}) collective-permute-start(bf16[256,128]{1,0:T(8,128)(2,1)S(1)} %copy-done.2), channel_id=1, source_target_pairs={{0,2},{1,3},{2,4},{3,5},{4,6},{5,7},{6,64},{7,65},{64,66},{65,67},... | collective-permute-start | bytes 196616 | tf_op jit(solution)/shard_map/ppermute | solution.py:14
  47.8 7.1 %collective-permute-start.7 = (bf16[256,128]{1,0:T(8,128)(2,1)S(1)}, bf16[256,128]{1,0:T(8,128)(2,1)S(1)}, u32[]{:S(2)}, u32[]{:S(2)}) collective-permute-start(bf16[256,128]{1,0:T(8,128)(2,1)S(1)} %copy-done.2), channel_id=1, source_target_pairs={{0,1},{1,2},{2,3},{3,4},{4,5},{5,6},{6,7},{7,64},{64,65},{65,66},{... | collective-permute-start | bytes 196616 | tf_op jit(solution)/shard_map/ppermute | solution.py:14
  139.0 2.9 %copy-start.1 = (bf16[8,256,128]{1,2,0:T(8,128)(2,1)S(1)}, bf16[8,256,128]{1,2,0:T(8,128)(2,1)}, u32[]{:S(2)}) copy-start(bf16[8,256,128]{1,2,0:T(8,128)(2,1)} %get-tuple-element.77) | copy-start | bytes 1572868
  143.0 13.4 %collective-permute-start.12 = (f32[256,128]{1,0:T(8,128)S(1)}, f32[256,128]{1,0:T(8,128)S(1)}, u32[]{:S(2)}, u32[]{:S(2)}) collective-permute-start(f32[256,128]{1,0:T(8,128)S(1)} %get-tuple-element.171), channel_id=1, source_target_pairs={{1,0},{2,1},{3,2},{4,3},{5,4},{6,5},{7,6},{64,7},{65,64},{66,65},{... | collective-permute-start | bytes 393224 | tf_op jit(solution)/shard_map/ppermute | solution.py:14
  144.9 16.3 %collective-permute-start.15 = (f32[256,128]{1,0:T(8,128)S(1)}, f32[256,128]{1,0:T(8,128)S(1)}, u32[]{:S(2)}, u32[]{:S(2)}) collective-permute-start(f32[256,128]{1,0:T(8,128)S(1)} %get-tuple-element.172), channel_id=1, source_target_pairs={{4,0},{5,1},{6,2},{7,3},{64,4},{65,5},{66,6},{67,7},{68,64},{69,65... | collective-permute-start | bytes 393224 | tf_op jit(solution)/shard_map/ppermute | solution.py:14
  146.8 17.9 %collective-permute-start.14 = (f32[256,128]{1,0:T(8,128)S(1)}, f32[256,128]{1,0:T(8,128)S(1)}, u32[]{:S(2)}, u32[]{:S(2)}) collective-permute-start(f32[256,128]{1,0:T(8,128)S(1)} %get-tuple-element.173), channel_id=1, source_target_pairs={{3,0},{4,1},{5,2},{6,3},{7,4},{64,5},{65,6},{66,7},{67,64},{68,65}... | collective-permute-start | bytes 393224 | tf_op jit(solution)/shard_map/ppermute | solution.py:14
  152.2 53.9 %collective-permute-start.13 = (f32[256,128]{1,0:T(8,128)S(1)}, f32[256,128]{1,0:T(8,128)S(1)}, u32[]{:S(2)}, u32[]{:S(2)}) collective-permute-start(f32[256,128]{1,0:T(8,128)S(1)} %get-tuple-element.174), channel_id=1, source_target_pairs={{2,0},{3,1},{4,2},{5,3},{6,4},{7,5},{64,6},{65,7},{66,64},{67,65},... | collective-permute-start | bytes 393224 | tf_op jit(solution)/shard_map/ppermute | solution.py:14
  154.2 52.6 %collective-permute-start.8 = (f32[256,128]{1,0:T(8,128)S(1)}, f32[256,128]{1,0:T(8,128)S(1)}, u32[]{:S(2)}, u32[]{:S(2)}) collective-permute-start(f32[256,128]{1,0:T(8,128)S(1)} %get-tuple-element.175), channel_id=1, source_target_pairs={{1,0},{2,1},{3,2},{4,3},{5,4},{6,5},{7,6},{64,7},{65,64},{66,65},{... | collective-permute-start | bytes 393224 | tf_op jit(solution)/shard_map/ppermute | solution.py:14
  156.4 50.4 %collective-permute-start.11 = (f32[256,128]{1,0:T(8,128)S(1)}, f32[256,128]{1,0:T(8,128)S(1)}, u32[]{:S(2)}, u32[]{:S(2)}) collective-permute-start(f32[256,128]{1,0:T(8,128)S(1)} %get-tuple-element.176), channel_id=1, source_target_pairs={{4,0},{5,1},{6,2},{7,3},{64,4},{65,5},{66,6},{67,7},{68,64},{69,65... | collective-permute-start | bytes 393224 | tf_op jit(solution)/shard_map/ppermute | solution.py:14
  161.2 45.5 %collective-permute-start.10 = (f32[256,128]{1,0:T(8,128)S(1)}, f32[256,128]{1,0:T(8,128)S(1)}, u32[]{:S(2)}, u32[]{:S(2)}) collective-permute-start(f32[256,128]{1,0:T(8,128)S(1)} %get-tuple-element.177), channel_id=1, source_target_pairs={{3,0},{4,1},{5,2},{6,3},{7,4},{64,5},{65,6},{66,7},{67,64},{68,65}... | collective-permute-start | bytes 393224 | tf_op jit(solution)/shard_map/ppermute | solution.py:14
  164.7 49.1 %collective-permute-start.9 = (f32[256,128]{1,0:T(8,128)S(1)}, f32[256,128]{1,0:T(8,128)S(1)}, u32[]{:S(2)}, u32[]{:S(2)}) collective-permute-start(f32[256,128]{1,0:T(8,128)S(1)} %get-tuple-element.178), channel_id=1, source_target_pairs={{2,0},{3,1},{4,2},{5,3},{6,4},{7,5},{64,6},{65,7},{66,64},{67,65},... | collective-permute-start | bytes 393224 | tf_op jit(solution)/shard_map/ppermute | solution.py:14
where the time goes:
time: 216 us; the launch traced here: 215 us
  starting transfers between devices  62 us (29%)
  matrix products  61.9 us (29%)
  waiting for transfers between devices  57.8 us (27%)
  other arithmetic  25.1 us (12%)
  local copies, waits for them, and re-layouts  6.44 us (3%)
    ppermute x16, starting transfers between devices, passed_along(): return lax.ppermute(value, axis, pairs)  62 us
    ppermute x16, waiting for transfers between devices, passed_along(): return lax.ppermute(value, axis, pairs)  57.8 us
    dot_general x8, matrix products, attend(): jnp.einsum('gqk,qgd->kd', dscore, qh, preferred_element_type=jnp.float32)  16.1 us
    dot_general x8, matrix products, attend(): jnp.einsum('qgd,kd->gqk', qh, kh, preferred_element_type=jnp.float32)  15.9 us
    dot_general x8, matrix products, attend(): jnp.einsum('gqk,kd->qgd', dscore, kh, preferred_element_type=jnp.float32)  15.3 us
    dot_general x8, matrix products, attend(): jnp.einsum('gqk,qgd->kd', probs, gh, preferred_element_type=jnp.float32)  9.48 us
    convert_element_type x8, other arithmetic, attend(): probs = (weights / total[..., None]).astype(jnp.bfloat16)  8.61 us
    reduce_sum x8, other arithmetic, attend(): total = jnp.sum(weights, axis=-1)  8.11 us
  transfers between devices with their start and end apart: 16, of which 5 were waited for; matrix products, arithmetic and copies ran while one was open for 2% of the time, Pallas kernels for 0%

commit v1 on v0

v1 whole, which is shorter than its diff:
```python
import functools
import math

import jax
import jax.numpy as jnp
from jax import lax
from jax.experimental import pallas as pl
from jax.experimental.pallas import tpu as pltpu
from jax.sharding import PartitionSpec as P

HEAD = 128
TILE = 128
SLOTS = 9
AHEAD = 7
NEG = -1e30
F32 = jnp.float32
BF16 = jnp.bfloat16


VALUE_STEPS = (
    ("part", 0), ("back", 0), ("part", 1), ("back", 1), ("move", 5), ("part", 2), ("back", 2),
    ("move", 6), ("part", 7), ("part", 3), ("back", 3), ("move", 3), ("dprob", 7), ("part", 8),
    ("part", 4), ("back", 4), ("move", 4), ("dprob", 8), ("part", 5), ("back", 5), ("move", 1),
    ("dprob", 5), ("part", 6), ("back", 6), ("move", 2), ("dprob", 6), ("dprob", 3), ("dprob", 4),
    ("back", 7), ("back", 8), ("dprob", 1), ("dprob", 2), ("move", 0), ("dprob", 0),
)
KEY_STEPS = (
    ("part", 0), ("back", 0), ("part", 1), ("back", 1), ("part", 2), ("back", 2), ("part", 3),
    ("part", 4), ("back", 3), ("part", 5), ("part", 6), ("back", 4), ("part", 7), ("part", 8),
    ("back", 5), ("query", 0), ("back", 6), ("query", 1), ("back", 7), ("back", 8),
)


def kernel(
    tiles_hbm, pads_hbm, q_hbm, k_hbm, v_hbm, g_hbm,
    dq_out, dk_out, dv_out,
    tiles_ref, pads_ref, q, g, qt, gt, kw, vw, kt, e, p, m_ref, l_ref, f_ref, d_ref, sv, rv, sk, rk,
    local_sem, kss, krs, vss, vrs, svs, rvs, sks, rks,
):
    ctx, grp = lax.axis_index("ctx"), lax.axis_index("grp")
    nctx, ngrp = lax.axis_size("ctx"), lax.axis_size("grp")
    heads = q_hbm.shape[1] // HEAD
    cols = heads * TILE
    pairs = heads // 2
    scale = 1.0 / math.sqrt(HEAD)
    c2 = scale * math.log2(math.e)
    mine = ctx * ngrp + grp
    up_grp = lax.rem(grp + 1, ngrp)
    up_ctx = lax.rem(ctx + jnp.where(grp == ngrp - 1, 1, 0), nctx)
    dn_grp = lax.rem(grp + ngrp - 1, ngrp)
    dn_ctx = lax.rem(ctx + jnp.where(grp == 0, nctx - 1, 0), nctx)
    nxt = {"ctx": up_ctx, "grp": up_grp}
    prv = {"ctx": dn_ctx, "grp": dn_grp}

    own = pl.ds(AHEAD * TILE, 2 * TILE)
    loads = [
        pltpu.make_async_copy(src, dst, local_sem.at[n])
        for n, (src, dst) in enumerate(
            (
                (k_hbm, kw.at[own]), (q_hbm, q), (v_hbm, vw.at[own]), (g_hbm, g),
                (tiles_hbm, tiles_ref), (pads_hbm, pads_ref),
            )
        )
    ]
    for load in loads:
        load.start()

    barrier = pltpu.get_barrier_semaphore()
    for other in (nxt, prv):
        pl.semaphore_signal(barrier, inc=1, device_id=other, device_id_type=pl.DeviceIdType.MESH)
    pl.semaphore_wait(barrier, 2)

    def ahead(win, ssem, rsem, dst):
        return pltpu.make_async_remote_copy(
            src_ref=win.at[pl.ds((dst + 2) * TILE, TILE)],
            dst_ref=win.at[pl.ds(dst * TILE, TILE)],
            send_sem=ssem.at[dst],
            recv_sem=rsem.at[dst],
            device_id=nxt,
            device_id_type=pl.DeviceIdType.MESH,
        )

    def back(sbuf, rbuf, ssem, rsem, slot):
        return pltpu.make_async_remote_copy(
            src_ref=sbuf.at[slot],
            dst_ref=rbuf.at[slot],
            send_sem=ssem.at[slot],
            recv_sem=rsem.at[slot],
            device_id=prv,
            device_id_type=pl.DeviceIdType.MESH,
        )

    k_move = [ahead(kw, kss, krs, dst) for dst in range(AHEAD)]
    v_move = [ahead(vw, vss, vrs, dst) for dst in range(AHEAD)]
    v_back = [back(sv, rv, svs, rvs, slot) for slot in range(AHEAD)]
    k_back = [back(sk, rk, sks, rks, slot) for slot in range(AHEAD)]

    loads[0].wait()
    k_move[5].start()
    k_move[6].start()

    loads[4].wait()
    loads[5].wait()
    first = [jnp.int32(0), jnp.int32(0)]
    stop = [jnp.int32(0), jnp.int32(0)]
    at = jnp.int32(0)
    for j in range(tiles_ref.shape[0]):
        after = at + tiles_ref[j]
        end = after * TILE - pads_ref[j]
        for i in range(2):
            tile = 2 * mine + i
            inside = (at <= tile) & (tile < after)
            first[i] = jnp.where(inside, at, first[i])
            stop[i] = jnp.where(inside, end, stop[i])
        at = after

    def rows_of(slot):
        return pl.ds(slot * TILE, TILE)

    def cols_of(i, c):
        return pl.ds(pl.multiple_of(i * cols + c * 2 * TILE, TILE), 2 * TILE)

    def two_heads(ref, i, c):
        at_row = pl.ds(i * TILE, TILE)
        return jnp.concatenate(
            [
                ref[at_row, pl.ds(pl.multiple_of((2 * c + n) * HEAD, HEAD), HEAD)]
                for n in range(2)
            ],
            axis=0,
        )

    def tiles_of(slot):
        return [i for i in range(2) if i <= slot <= AHEAD + i]

    def over_pairs(body, init=0):
        return lax.fori_loop(0, pairs, body, init, unroll=True)

    def scores(slot):
        def step(c, carry):
            key = kw[rows_of(slot)]
            for i in tiles_of(slot):
                s = jnp.dot(key, qt[:, cols_of(i, c)], preferred_element_type=F32)
                if slot == AHEAD + i:
                    row = lax.broadcasted_iota(jnp.int32, s.shape, 0)
                    col = lax.broadcasted_iota(jnp.int32, s.shape, 1)
                    s = jnp.where(row <= (col & (TILE - 1)), s, NEG)
                top = jnp.max(s, axis=0, keepdims=True) * c2
                w = jnp.exp2(s * c2 - top)
                e[rows_of(slot), cols_of(i, c)] = w
                m_ref[pl.ds(slot, 1), cols_of(i, c)] = top
                l_ref[pl.ds(slot, 1), cols_of(i, c)] = jnp.sum(w, axis=0, keepdims=True)
            return carry

        over_pairs(step)
        kt[:, rows_of(slot)] = jnp.transpose(kw[rows_of(slot)])

    def factors():
        for i in range(2):
            part = pl.ds(i * cols, cols)
            shape = (16, cols)
            row = lax.broadcasted_iota(jnp.int32, shape, 0)
            token = lax.broadcasted_iota(jnp.int32, shape, 1) & (TILE - 1)
            tile = 2 * mine + i
            valid = (row >= i) & (row <= AHEAD + i) & (row + (2 * mine - AHEAD) >= first[i])
            tops = jnp.where(valid, m_ref[:, part], NEG)
            w = jnp.exp2(tops - jnp.max(tops, axis=0, keepdims=True))
            total = jnp.sum(w * jnp.where(valid, l_ref[:, part], 0.0), axis=0, keepdims=True)
            live = token < stop[i] - tile * TILE
            f_ref[:, part] = jnp.where(live, w / total, 0.0)

    def value_part(slot):
        def step(c, acc):
            for i in tiles_of(slot):
                w = e[rows_of(slot), cols_of(i, c)] * f_ref[pl.ds(slot, 1), cols_of(i, c)]
                w = w.astype(BF16)
                p[rows_of(slot), cols_of(i, c)] = w
                acc = acc + jnp.dot(w, two_heads(g, i, c), preferred_element_type=F32)
            return acc

        return over_pairs(step, jnp.zeros((TILE, HEAD), F32))

    def dprobs(slot):
        def step(c, carry):
            value = vw[rows_of(slot)]
            for i in tiles_of(slot):
                d = jnp.dot(value, gt[:, cols_of(i, c)], preferred_element_type=F32)
                e[rows_of(slot), cols_of(i, c)] = d
                d = d * p[rows_of(slot), cols_of(i, c)].astype(F32)
                d_ref[pl.ds(slot, 1), cols_of(i, c)] = jnp.sum(d, axis=0, keepdims=True)
            return carry

        over_pairs(step)

    def deltas():
        for i in range(2):
            part = pl.ds(i * cols, cols)
            row = lax.broadcasted_iota(jnp.int32, (16, cols), 0)
            terms = jnp.where((row >= i) & (row <= AHEAD + i), d_ref[:, part], 0.0)
            f_ref[:, part] = jnp.broadcast_to(jnp.sum(terms, axis=0, keepdims=True), (16, cols))

    def key_part(slot):
        def step(c, acc):
            for i in tiles_of(slot):
                d = e[rows_of(slot), cols_of(i, c)] - f_ref[pl.ds(0, 1), cols_of(i, c)]
                d = (p[rows_of(slot), cols_of(i, c)].astype(F32) * d).astype(BF16)
                p[rows_of(slot), cols_of(i, c)] = d
                acc = acc + jnp.dot(d, two_heads(q, i, c), preferred_element_type=F32)
            return acc

        return over_pairs(step, jnp.zeros((TILE, HEAD), F32)) * scale

    def query_part(i, dq):
        window = pl.ds(i * TILE, (SLOTS - 1) * TILE)

        def step(c, carry):
            t = jnp.dot(kt[:, window], p[window, cols_of(i, c)], preferred_element_type=F32) * scale
            for n in range(2):
                head = pl.ds(pl.multiple_of((2 * c + n) * HEAD, HEAD), HEAD)
                t_head = t[:, n * TILE : (n + 1) * TILE]
                dq[pl.ds(i * TILE, TILE), head] = jnp.transpose(t_head).astype(BF16)
            return carry

        over_pairs(step)

    def returned(part, slot, moves, sbuf, rbuf, out):
        if slot >= 2:
            moves[slot - 2].wait_recv()
            part = part + rbuf[slot - 2].astype(F32)
        if slot < AHEAD:
            sbuf[slot] = part.astype(BF16)
            moves[slot].start()
        else:
            out[pl.ds((slot - AHEAD) * TILE, TILE), :] = part.astype(BF16)

    def passed_on(moves, slot):
        moves[slot].wait_recv()
        if slot >= 2:
            moves[slot - 2].start()

    def turned(ref, out):
        def step(c, carry):
            for i in range(2):
                for n in range(2):
                    head = pl.ds(pl.multiple_of((2 * c + n) * HEAD, HEAD), HEAD)
                    at_col = pl.ds(pl.multiple_of(i * cols + (2 * c + n) * TILE, TILE), TILE)
                    out[:, at_col] = jnp.transpose(ref[pl.ds(i * TILE, TILE), head])
            return carry

        over_pairs(step)

    loads[1].wait()
    turned(q, qt)
    loads[3].wait()
    turned(g, gt)
    for slot, done in ((5, 7), (6, 8), (3, 5), (4, 6), (1, 3), (2, 4)):
        passed_on(k_move, slot)
        if slot == 2:
            loads[2].wait()
            v_move[5].start()
            v_move[6].start()
        scores(done)
    scores(1)
    scores(2)
    passed_on(k_move, 0)
    scores(0)
    factors()

    parts = {}
    for what, slot in VALUE_STEPS:
        if what == "part":
            parts[slot] = value_part(slot)
        elif what == "back":
            returned(parts.pop(slot), slot, v_back, sv, rv, dv_out)
        elif what == "move":
            passed_on(v_move, slot)
        else:
            dprobs(slot)
    deltas()

    for what, slot in KEY_STEPS:
        if what == "part":
            parts[slot] = key_part(slot)
        elif what == "back":
            returned(parts.pop(slot), slot, k_back, sk, rk, dk_out)
        else:
            query_part(slot, dq_out)

    for moves in (k_move, v_move, v_back, k_back):
        for move in moves:
            move.wait_send()


def shards(queries, keys, values, output_gradient, doc_tiles, doc_pads):
    rows, wide = queries.shape
    window = SLOTS * TILE
    both = 2 * (wide // HEAD) * TILE
    anywhere = pl.BlockSpec(memory_space=pl.ANY)
    vmem = pl.BlockSpec(memory_space=pltpu.VMEM)
    dma = pltpu.SemaphoreType.DMA
    operands = (doc_tiles, doc_pads, queries, keys, values, output_gradient)
    return pl.pallas_call(
        kernel,
        out_shape=(
            jax.ShapeDtypeStruct((rows, wide), BF16),
            jax.ShapeDtypeStruct(keys.shape, BF16),
            jax.ShapeDtypeStruct(values.shape, BF16),
        ),
        in_specs=[anywhere] * 6,
        out_specs=(vmem, vmem, vmem),
        scratch_shapes=[
            pltpu.SMEM(doc_tiles.shape, jnp.int32),
            pltpu.SMEM(doc_pads.shape, jnp.int32),
            pltpu.VMEM((rows, wide), BF16),
            pltpu.VMEM((rows, wide), BF16),
            pltpu.VMEM((HEAD, both), BF16),
            pltpu.VMEM((HEAD, both), BF16),
            pltpu.VMEM((window, HEAD), BF16),
            pltpu.VMEM((window, HEAD), BF16),
            pltpu.VMEM((HEAD, window), BF16),
            pltpu.VMEM((window, both), F32),
            pltpu.VMEM((window, both), BF16),
            pltpu.VMEM((16, both), F32),
            pltpu.VMEM((16, both), F32),
            pltpu.VMEM((16, both), F32),
            pltpu.VMEM((16, both), F32),
        ]
        + [pltpu.VMEM((AHEAD, TILE, HEAD), BF16)] * 4
        + [dma((6,))]
        + [dma((AHEAD,))] * 8,
        compiler_params=pltpu.CompilerParams(
            collective_id=0, has_side_effects=True, vmem_limit_bytes=48 * 1024 * 1024
        ),
        cost_estimate=pl.CostEstimate(flops=2_700_000_000, bytes_accessed=2_400_000, transcendentals=2_100_000),
        name="attention_backward",
    )(*[pltpu.with_memory_space_constraint(x, pltpu.HBM) for x in operands])


def solution(mesh):
    split = P(("ctx", "grp"), "tp")
    return jax.shard_map(
        shards,
        mesh=mesh,
        in_specs=(split, split, split, split, P(), P()),
        out_specs=(split, split, split),
        check_vma=False,
    )
```

time: 216 us -> 59.2 us (0.27)
  the two profiles are of different devices: /device:TPU:197 before, /device:TPU:2 now
where the time goes in v1:
time: 59.2 us; the launch traced here: 59.1 us
  Pallas kernels  56.4 us (95%)
  local copies, waits for them, and re-layouts  2.05 us (3%)
  between operations  0.64 us (1%)
    pallas_call x1, Pallas kernels, shards(): pl.pallas_call(kernel, out_shape=(jax.ShapeDtypeStruct((rows, wide), BF16...  56.4 us
    unnamed x3, local copies, waits for them, and re-layouts  2.05 us

profile of v1, /device:TPU:2, one launch (start us, length us, event | category | flops | bytes accessed | tf_op | source)
XLA Modules:
  0.0 59.1 jit_solution(7104978545968632406)
XLA Ops:
  0.6 56.4 %attention_backward.1 = (bf16[256,1024]{1,0:T(8,128)(2,1)S(1)}, bf16[256,128]{1,0:T(8,128)(2,1)S(1)}, bf16[256,128]{1,0:T(8,128)(2,1)S(1)}) custom-call(s32[32]{0:T(128)} %tiles_hbm.1, s32[32]{0:T(128)} %pads_hbm.1, bf16[256,1024]{1,0:T(8,128)(2,1)} %q_hbm.1, bf16[256,128]{1,0:T(8,128)(2,1)} %k_hbm.1, bf16[256,128]{1,0:T(8,128)(2,1)} %v_hbm.1, ...), custom_call_target="tpu_custom_call" | custom-call | flops 2700000000 | bytes 2400000 | tf_op jit(solution)/shard_map/attention_backward/pallas_call | solution.py:302
  57.0 0.8 %copy.12 = bf16[256,1024]{1,0:T(8,128)(2,1)} copy(bf16[256,1024]{1,0:T(8,128)(2,1)S(1)} %get-tuple-element.6) | data formatting | bytes 1048576
  57.8 0.6 %copy.13 = bf16[256,128]{1,0:T(8,128)(2,1)} copy(bf16[256,128]{1,0:T(8,128)(2,1)S(1)} %get-tuple-element.7) | data formatting | bytes 131072
  58.5 0.6 %copy.14 = bf16[256,128]{1,0:T(8,128)(2,1)} copy(bf16[256,128]{1,0:T(8,128)(2,1)S(1)} %get-tuple-element.8) | data formatting | bytes 131072

commit v2 on v1

--- a/solution.py
+++ b/solution.py
@@ -17,18 +17,8 @@
 BF16 = jnp.bfloat16
 
 
-VALUE_STEPS = (
-    ("part", 0), ("back", 0), ("part", 1), ("back", 1), ("move", 5), ("part", 2), ("back", 2),
-    ("move", 6), ("part", 7), ("part", 3), ("back", 3), ("move", 3), ("dprob", 7), ("part", 8),
-    ("part", 4), ("back", 4), ("move", 4), ("dprob", 8), ("part", 5), ("back", 5), ("move", 1),
-    ("dprob", 5), ("part", 6), ("back", 6), ("move", 2), ("dprob", 6), ("dprob", 3), ("dprob", 4),
-    ("back", 7), ("back", 8), ("dprob", 1), ("dprob", 2), ("move", 0), ("dprob", 0),
-)
-KEY_STEPS = (
-    ("part", 0), ("back", 0), ("part", 1), ("back", 1), ("part", 2), ("back", 2), ("part", 3),
-    ("part", 4), ("back", 3), ("part", 5), ("part", 6), ("back", 4), ("part", 7), ("part", 8),
-    ("back", 5), ("query", 0), ("back", 6), ("query", 1), ("back", 7), ("back", 8),
-)
+BACK = (4, 3, 3, 2, 2, 1, 1)
+HOME = (4, 1, 1, 2, 2, 1, 1)
 
 
 def kernel(
@@ -45,12 +35,11 @@
     scale = 1.0 / math.sqrt(HEAD)
     c2 = scale * math.log2(math.e)
     mine = ctx * ngrp + grp
-    up_grp = lax.rem(grp + 1, ngrp)
-    up_ctx = lax.rem(ctx + jnp.where(grp == ngrp - 1, 1, 0), nctx)
-    dn_grp = lax.rem(grp + ngrp - 1, ngrp)
-    dn_ctx = lax.rem(ctx + jnp.where(grp == 0, nctx - 1, 0), nctx)
-    nxt = {"ctx": up_ctx, "grp": up_grp}
-    prv = {"ctx": dn_ctx, "grp": dn_grp}
+    shards_all = nctx * ngrp
+
+    def shard(distance):
+        index = mine + distance
+        return {"ctx": index // ngrp, "grp": index % ngrp}
 
     own = pl.ds(AHEAD * TILE, 2 * TILE)
     loads = [
@@ -65,39 +54,77 @@
     for load in loads:
         load.start()
 
+    @pl.when(mine < 4)
+    def _():
+        kw[pl.ds(0, AHEAD * TILE)] = jnp.zeros((AHEAD * TILE, HEAD), BF16)
+        vw[pl.ds(0, AHEAD * TILE)] = jnp.zeros((AHEAD * TILE, HEAD), BF16)
+
+    @pl.when(mine >= shards_all - 4)
+    def _():
+        rv[...] = jnp.zeros(rv.shape, BF16)
+        rk[...] = jnp.zeros(rk.shape, BF16)
+
     barrier = pltpu.get_barrier_semaphore()
-    for other in (nxt, prv):
-        pl.semaphore_signal(barrier, inc=1, device_id=other, device_id_type=pl.DeviceIdType.MESH)
-    pl.semaphore_wait(barrier, 2)
+    partners = jnp.int32(0)
+    for distance in (1, 2, 4):
+        for to, there in ((distance, mine + distance < shards_all), (-distance, mine >= distance)):
+            @pl.when(there)
+            def _():
+                pl.semaphore_signal(
+                    barrier, inc=1, device_id=shard(to), device_id_type=pl.DeviceIdType.MESH
+                )
+            partners = partners + jnp.where(there, 1, 0)
+    pl.semaphore_wait(barrier, partners)
+
+    class Move:
+        def __init__(self, src, dst, ssem, rsem, to, sends, receives):
+            self.copy = pltpu.make_async_remote_copy(
+                src_ref=src, dst_ref=dst, send_sem=ssem, recv_sem=rsem,
+                device_id=shard(to), device_id_type=pl.DeviceIdType.MESH,
+            )
+            self.sends, self.receives = sends, receives
+
+        def start(self):
+            pl.when(self.sends)(self.copy.start)
+
+        def wait_send(self):
+            pl.when(self.sends)(self.copy.wait_send)
+
+        def wait_recv(self):
+            pl.when(self.receives)(self.copy.wait_recv)
 
     def ahead(win, ssem, rsem, dst):
-        return pltpu.make_async_remote_copy(
-            src_ref=win.at[pl.ds((dst + 2) * TILE, TILE)],
-            dst_ref=win.at[pl.ds(dst * TILE, TILE)],
-            send_sem=ssem.at[dst],
-            recv_sem=rsem.at[dst],
-            device_id=nxt,
-            device_id_type=pl.DeviceIdType.MESH,
+        back = BACK[dst]
+        step = 1 if back == 3 else back
+        src = dst + 2 if back == 3 else (AHEAD + 1 if dst % 2 == 0 else AHEAD)
+        sends = mine + step < shards_all
+        if back == 3:
+            sends = sends & (mine >= 2)
+        return Move(
+            win.at[pl.ds(src * TILE, TILE)], win.at[pl.ds(dst * TILE, TILE)],
+            ssem.at[dst], rsem.at[dst], step, sends, mine >= back,
         )
 
-    def back(sbuf, rbuf, ssem, rsem, slot):
-        return pltpu.make_async_remote_copy(
-            src_ref=sbuf.at[slot],
-            dst_ref=rbuf.at[slot],
-            send_sem=ssem.at[slot],
-            recv_sem=rsem.at[slot],
-            device_id=prv,
-            device_id_type=pl.DeviceIdType.MESH,
+    def home(sbuf, rbuf, ssem, rsem, slot):
+        receives = mine + HOME[slot] < shards_all
+        if BACK[slot] == 3:
+            receives = receives & (mine >= 2)
+        return Move(
+            sbuf.at[slot], rbuf.at[slot], ssem.at[slot], rsem.at[slot],
+            -HOME[slot], mine >= BACK[slot], receives,
         )
 
     k_move = [ahead(kw, kss, krs, dst) for dst in range(AHEAD)]
     v_move = [ahead(vw, vss, vrs, dst) for dst in range(AHEAD)]
-    v_back = [back(sv, rv, svs, rvs, slot) for slot in range(AHEAD)]
-    k_back = [back(sk, rk, sks, rks, slot) for slot in range(AHEAD)]
+    v_home = [home(sv, rv, svs, rvs, slot) for slot in range(AHEAD)]
+    k_home = [home(sk, rk, sks, rks, slot) for slot in range(AHEAD)]
 
     loads[0].wait()
-    k_move[5].start()
-    k_move[6].start()
+    for slot in (3, 4, 5, 6, 0):
+        k_move[slot].start()
+    loads[2].wait()
+    for slot in (3, 4):
+        v_move[slot].start()
 
     loads[4].wait()
     loads[5].wait()
@@ -223,21 +250,6 @@
 
         over_pairs(step)
 
-    def returned(part, slot, moves, sbuf, rbuf, out):
-        if slot >= 2:
-            moves[slot - 2].wait_recv()
-            part = part + rbuf[slot - 2].astype(F32)
-        if slot < AHEAD:
-            sbuf[slot] = part.astype(BF16)
-            moves[slot].start()
-        else:
-            out[pl.ds((slot - AHEAD) * TILE, TILE), :] = part.astype(BF16)
-
-    def passed_on(moves, slot):
-        moves[slot].wait_recv()
-        if slot >= 2:
-            moves[slot - 2].start()
-
     def turned(ref, out):
         def step(c, carry):
             for i in range(2):
@@ -249,44 +261,85 @@
 
         over_pairs(step)
 
+    def arrived(moves, *slots):
+        for slot in slots:
+            moves[slot].wait_recv()
+
+    def relayed(moves):
+        for slot in (3, 4):
+            moves[slot].wait_recv()
+            moves[slot - 2].start()
+
+    def sent(part, slot, moves, sbuf):
+        sbuf[slot] = part.astype(BF16)
+        moves[slot].start()
+
+    def added(part, slot, moves, sbuf, rbuf):
+        moves[slot - 2].wait_recv()
+        sent(part + rbuf[slot - 2].astype(F32), slot, moves, sbuf)
+
+    def settled(parts, moves, rbuf, out):
+        for slot in (7, 8):
+            part = parts[slot]
+            for came in (slot - 2, slot - 4) + ((0,) if slot == 8 else ()):
+                moves[came].wait_recv()
+                part = part + rbuf[came].astype(F32)
+            out[pl.ds((slot - AHEAD) * TILE, TILE), :] = part.astype(BF16)
+
     loads[1].wait()
     turned(q, qt)
+    scores(7)
+    scores(8)
+    relayed(k_move)
+    for slot in (5, 6, 0):
+        v_move[slot].start()
     loads[3].wait()
     turned(g, gt)
-    for slot, done in ((5, 7), (6, 8), (3, 5), (4, 6), (1, 3), (2, 4)):
-        passed_on(k_move, slot)
-        if slot == 2:
-            loads[2].wait()
-            v_move[5].start()
-            v_move[6].start()
-        scores(done)
+    arrived(k_move, 5, 6)
+    for slot in (5, 6, 3, 4):
+        scores(slot)
+    relayed(v_move)
+    arrived(k_move, 0)
+    scores(0)
+    arrived(k_move, 1)
     scores(1)
+    arrived(k_move, 2)
     scores(2)
-    passed_on(k_move, 0)
-    scores(0)
     factors()
 
-    parts = {}
-    for what, slot in VALUE_STEPS:
-        if what == "part":
-            parts[slot] = value_part(slot)
-        elif what == "back":
-            returned(parts.pop(slot), slot, v_back, sv, rv, dv_out)
-        elif what == "move":
-            passed_on(v_move, slot)
-        else:
-            dprobs(slot)
+    v_part = {}
+    for slot in (1, 2, 0, 5, 6):
+        sent(value_part(slot), slot, v_home, sv)
+    for slot in (3, 4, 7, 8):
+        v_part[slot] = value_part(slot)
+    dprobs(7)
+    dprobs(8)
+    arrived(v_move, 5, 6)
+    for slot in (5, 6, 3, 4):
+        dprobs(slot)
+    arrived(v_move, 0)
+    dprobs(0)
+    added(v_part[3], 3, v_home, sv, rv)
+    added(v_part[4], 4, v_home, sv, rv)
+    arrived(v_move, 1)
+    dprobs(1)
+    arrived(v_move, 2)
+    dprobs(2)
     deltas()
 
-    for what, slot in KEY_STEPS:
-        if what == "part":
-            parts[slot] = key_part(slot)
-        elif what == "back":
-            returned(parts.pop(slot), slot, k_back, sk, rk, dk_out)
-        else:
-            query_part(slot, dq_out)
-
-    for moves in (k_move, v_move, v_back, k_back):
+    k_part = {}
+    for slot in (1, 2, 0, 5, 6):
+        sent(key_part(slot), slot, k_home, sk)
+    for slot in (3, 4, 7, 8):
+        k_part[slot] = key_part(slot)
+    query_part(0, dq_out)
+    added(k_part[3], 3, k_home, sk, rk)
+    added(k_part[4], 4, k_home, sk, rk)
+    query_part(1, dq_out)
+    settled(v_part, v_home, rv, dv_out)
+    settled(k_part, k_home, rk, dk_out)
+
+    for moves in (k_move, v_move, v_home, k_home):
         for move in moves:
             move.wait_send()
 

time: 59.2 us -> 43.6 us (0.74)
  the two profiles are of different devices: /device:TPU:2 before, /device:TPU:238 now
where the time goes in v2:
time: 43.6 us; the launch traced here: 43.5 us
  Pallas kernels  40.8 us (94%)
  local copies, waits for them, and re-layouts  2.05 us (5%)
  between operations  0.64 us (1%)
    pallas_call x1, Pallas kernels, shards(): pl.pallas_call(kernel, out_shape=(jax.ShapeDtypeStruct((rows, wide), BF16...  40.8 us
    unnamed x3, local copies, waits for them, and re-layouts  2.05 us

profile of v2, /device:TPU:238, one launch (start us, length us, event | category | flops | bytes accessed | tf_op | source)
XLA Modules:
  0.0 43.5 jit_solution(7371278744261720214)
XLA Ops:
  0.6 40.8 %attention_backward.1 = (bf16[256,1024]{1,0:T(8,128)(2,1)S(1)}, bf16[256,128]{1,0:T(8,128)(2,1)S(1)}, bf16[256,128]{1,0:T(8,128)(2,1)S(1)}) custom-call(s32[32]{0:T(128)} %tiles_hbm.1, s32[32]{0:T(128)} %pads_hbm.1, bf16[256,1024]{1,0:T(8,128)(2,1)} %q_hbm.1, bf16[256,128]{1,0:T(8,128)(2,1)} %k_hbm.1, bf16[256,128]{1,0:T(8,128)(2,1)} %v_hbm.1, ...), custom_call_target="tpu_custom_call" | custom-call | flops 2700000000 | bytes 2400000 | tf_op jit(solution)/shard_map/attention_backward/pallas_call | solution.py:355
  41.4 0.8 %copy.12 = bf16[256,1024]{1,0:T(8,128)(2,1)} copy(bf16[256,1024]{1,0:T(8,128)(2,1)S(1)} %get-tuple-element.6) | data formatting | bytes 1048576
  42.2 0.6 %copy.13 = bf16[256,128]{1,0:T(8,128)(2,1)} copy(bf16[256,128]{1,0:T(8,128)(2,1)S(1)} %get-tuple-element.7) | data formatting | bytes 131072
  42.9 0.6 %copy.14 = bf16[256,128]{1,0:T(8,128)(2,1)} copy(bf16[256,128]{1,0:T(8,128)(2,1)S(1)} %get-tuple-element.8) | data formatting | bytes 131072

commit v3 on v2

--- a/solution.py
+++ b/solution.py
@@ -1,4 +1,3 @@
-import functools
 import math
 
 import jax
@@ -18,9 +17,6 @@
 
 
 BACK = (4, 3, 3, 2, 2, 1, 1)
-HOME = (4, 1, 1, 2, 2, 1, 1)
-
-
 def kernel(
     tiles_hbm, pads_hbm, q_hbm, k_hbm, v_hbm, g_hbm,
     dq_out, dk_out, dv_out,
@@ -66,7 +62,7 @@
 
     barrier = pltpu.get_barrier_semaphore()
     partners = jnp.int32(0)
-    for distance in (1, 2, 4):
+    for distance in (1, 2):
         for to, there in ((distance, mine + distance < shards_all), (-distance, mine >= distance)):
             @pl.when(there)
             def _():
@@ -94,37 +90,67 @@
             pl.when(self.receives)(self.copy.wait_recv)
 
     def ahead(win, ssem, rsem, dst):
-        back = BACK[dst]
-        step = 1 if back == 3 else back
-        src = dst + 2 if back == 3 else (AHEAD + 1 if dst % 2 == 0 else AHEAD)
-        sends = mine + step < shards_all
-        if back == 3:
-            sends = sends & (mine >= 2)
+        if BACK[dst] == 3:
+            src, step, sends = dst + 2, 1, (mine >= 2) & (mine + 1 < shards_all)
+        elif BACK[dst] == 1:
+            src, step, sends = dst - 2, -1, mine >= 2
+        elif BACK[dst] == 4:
+            src, step, sends = 4, 2, (mine >= 2) & (mine + 2 < shards_all)
+        else:
+            src, step, sends = dst + 4, 2, mine + 2 < shards_all
         return Move(
-            win.at[pl.ds(src * TILE, TILE)], win.at[pl.ds(dst * TILE, TILE)],
-            ssem.at[dst], rsem.at[dst], step, sends, mine >= back,
+            win.at[rows_of(src)], win.at[rows_of(dst)],
+            ssem.at[dst], rsem.at[dst], step, sends, mine >= BACK[dst],
+        )
+
+    def ahead_last(win, ssem, rsem, dst):
+        return Move(
+            win.at[rows_of(dst + 2)], win.at[rows_of(dst)],
+            ssem.at[dst - 2], rsem.at[dst], 1, mine == shards_all - 2, None,
         )
 
     def home(sbuf, rbuf, ssem, rsem, slot):
-        receives = mine + HOME[slot] < shards_all
         if BACK[slot] == 3:
-            receives = receives & (mine >= 2)
+            to, sends = -1, mine >= 3
+            receives = (mine >= 2) & (mine + 1 < shards_all)
+        elif BACK[slot] == 1:
+            to, sends, receives = 1, (mine >= 1) & (mine + 1 < shards_all), mine >= 2
+        elif BACK[slot] == 4:
+            to, sends = -2, mine >= 4
+            receives = (mine >= 2) & (mine + 2 < shards_all)
+        else:
+            to, sends, receives = -2, mine >= 2, mine + 1 < shards_all
         return Move(
-            sbuf.at[slot], rbuf.at[slot], ssem.at[slot], rsem.at[slot],
-            -HOME[slot], mine >= BACK[slot], receives,
-        )
+            sbuf.at[slot], rbuf.at[slot], ssem.at[slot], rsem.at[slot], to, sends, receives
+        )
+
+    def home_last(sbuf, rbuf, ssem, rsem, slot):
+        return Move(
+            sbuf.at[slot], rbuf.at[slot - 2], ssem.at[slot], rsem.at[slot - 2],
+            -1, mine == shards_all - 1, None,
+        )
+
+    def rows_of(slot):
+        return pl.ds(slot * TILE, TILE)
 
     k_move = [ahead(kw, kss, krs, dst) for dst in range(AHEAD)]
     v_move = [ahead(vw, vss, vrs, dst) for dst in range(AHEAD)]
     v_home = [home(sv, rv, svs, rvs, slot) for slot in range(AHEAD)]
     k_home = [home(sk, rk, sks, rks, slot) for slot in range(AHEAD)]
+    k_move_last = {slot: ahead_last(kw, kss, krs, slot) for slot in (5, 6)}
+    v_move_last = {slot: ahead_last(vw, vss, vrs, slot) for slot in (5, 6)}
+    v_home_last = {slot: home_last(sv, rv, svs, rvs, slot) for slot in (5, 6)}
+    k_home_last = {slot: home_last(sk, rk, sks, rks, slot) for slot in (5, 6)}
+
+    def launched(moves, last, *slots):
+        for slot in slots:
+            moves[slot].start()
+            if slot in (3, 4):
+                last[slot + 2].start()
 
     loads[0].wait()
-    for slot in (3, 4, 5, 6, 0):
-        k_move[slot].start()
+    launched(k_move, k_move_last, 3, 4)
     loads[2].wait()
-    for slot in (3, 4):
-        v_move[slot].start()
 
     loads[4].wait()
     loads[5].wait()
@@ -140,9 +166,6 @@
             first[i] = jnp.where(inside, at, first[i])
             stop[i] = jnp.where(inside, end, stop[i])
         at = after
-
-    def rows_of(slot):
-        return pl.ds(slot * TILE, TILE)
 
     def cols_of(i, c):
         return pl.ds(pl.multiple_of(i * cols + c * 2 * TILE, TILE), 2 * TILE)
@@ -269,72 +292,65 @@
         for slot in (3, 4):
             moves[slot].wait_recv()
             moves[slot - 2].start()
-
-    def sent(part, slot, moves, sbuf):
+            moves[slot + 2].start()
+        moves[0].start()
+
+    def sent(part, slot, moves, last, sbuf):
         sbuf[slot] = part.astype(BF16)
         moves[slot].start()
-
-    def added(part, slot, moves, sbuf, rbuf):
-        moves[slot - 2].wait_recv()
-        sent(part + rbuf[slot - 2].astype(F32), slot, moves, sbuf)
+        if slot in (5, 6):
+            last[slot].start()
+
+    def added(part, slot, moves, last, sbuf, rbuf):
+        for came in (1, 5) if slot == 3 else (2, 6, 0):
+            moves[came].wait_recv()
+            part = part + rbuf[came].astype(F32)
+        sent(part, slot, moves, last, sbuf)
 
     def settled(parts, moves, rbuf, out):
         for slot in (7, 8):
-            part = parts[slot]
-            for came in (slot - 2, slot - 4) + ((0,) if slot == 8 else ()):
-                moves[came].wait_recv()
-                part = part + rbuf[came].astype(F32)
-            out[pl.ds((slot - AHEAD) * TILE, TILE), :] = part.astype(BF16)
+            moves[slot - 4].wait_recv()
+            part = parts[slot] + rbuf[slot - 4].astype(F32)
+            out[rows_of(slot - AHEAD), :] = part.astype(BF16)
 
     loads[1].wait()
     turned(q, qt)
     scores(7)
     scores(8)
+    launched(v_move, v_move_last, 3, 4)
     relayed(k_move)
-    for slot in (5, 6, 0):
-        v_move[slot].start()
     loads[3].wait()
     turned(g, gt)
-    arrived(k_move, 5, 6)
-    for slot in (5, 6, 3, 4):
+    for slot in (3, 4):
         scores(slot)
     relayed(v_move)
-    arrived(k_move, 0)
-    scores(0)
-    arrived(k_move, 1)
-    scores(1)
-    arrived(k_move, 2)
-    scores(2)
+    for slot in (1, 5, 2, 6, 0):
+        arrived(k_move, slot)
+        scores(slot)
     factors()
 
     v_part = {}
-    for slot in (1, 2, 0, 5, 6):
-        sent(value_part(slot), slot, v_home, sv)
+    for slot in (1, 5, 2, 6, 0):
+        sent(value_part(slot), slot, v_home, v_home_last, sv)
     for slot in (3, 4, 7, 8):
         v_part[slot] = value_part(slot)
-    dprobs(7)
-    dprobs(8)
-    arrived(v_move, 5, 6)
-    for slot in (5, 6, 3, 4):
+    for slot in (7, 8, 3, 4):
         dprobs(slot)
-    arrived(v_move, 0)
-    dprobs(0)
-    added(v_part[3], 3, v_home, sv, rv)
-    added(v_part[4], 4, v_home, sv, rv)
-    arrived(v_move, 1)
-    dprobs(1)
-    arrived(v_move, 2)
-    dprobs(2)
+    for slot in (1, 5, 2, 6, 0):
+        arrived(v_move, slot)
+        dprobs(slot)
     deltas()
 
     k_part = {}
-    for slot in (1, 2, 0, 5, 6):
-        sent(key_part(slot), slot, k_home, sk)
+    for slot in (1, 5, 2, 6, 0):
+        sent(key_part(slot), slot, k_home, k_home_last, sk)
+    for slot in (3, 4):
+        added(v_part[slot], slot, v_home, v_home_last, sv, rv)
     for slot in (3, 4, 7, 8):
         k_part[slot] = key_part(slot)
     query_part(0, dq_out)
-    added(k_part[3], 3, k_home, sk, rk)
-    added(k_part[4], 4, k_home, sk, rk)
+    added(k_part[3], 3, k_home, k_home_last, sk, rk)
+    added(k_part[4], 4, k_home, k_home_last, sk, rk)
     query_part(1, dq_out)
     settled(v_part, v_home, rv, dv_out)
     settled(k_part, k_home, rk, dk_out)
@@ -342,6 +358,20 @@
     for moves in (k_move, v_move, v_home, k_home):
         for move in moves:
             move.wait_send()
+    for moves in (k_move_last, v_move_last, v_home_last, k_home_last):
+        for move in moves.values():
+            move.wait_send()
+
+
+def store(dq, dk, dv, dq_out, dk_out, dv_out, sem):
+    moves = [
+        pltpu.make_async_copy(src, dst, sem.at[n])
+        for n, (src, dst) in enumerate(((dq, dq_out), (dk, dk_out), (dv, dv_out)))
+    ]
+    for move in moves:
+        move.start()
+    for move in moves:
+        move.wait()
 
 
 def shards(queries, keys, values, output_gradient, doc_tiles, doc_pads):
@@ -352,13 +382,10 @@
     vmem = pl.BlockSpec(memory_space=pltpu.VMEM)
     dma = pltpu.SemaphoreType.DMA
     operands = (doc_tiles, doc_pads, queries, keys, values, output_gradient)
-    return pl.pallas_call(
+    shapes = tuple(jax.ShapeDtypeStruct(x.shape, BF16) for x in (queries, keys, values))
+    grads = pl.pallas_call(
         kernel,
-        out_shape=(
-            jax.ShapeDtypeStruct((rows, wide), BF16),
-            jax.ShapeDtypeStruct(keys.shape, BF16),
-            jax.ShapeDtypeStruct(values.shape, BF16),
-        ),
+        out_shape=shapes,
         in_specs=[anywhere] * 6,
         out_specs=(vmem, vmem, vmem),
         scratch_shapes=[
@@ -387,6 +414,14 @@
         cost_estimate=pl.CostEstimate(flops=2_700_000_000, bytes_accessed=2_400_000, transcendentals=2_100_000),
         name="attention_backward",
     )(*[pltpu.with_memory_space_constraint(x, pltpu.HBM) for x in operands])
+    return pl.pallas_call(
+        store,
+        out_shape=shapes,
+        in_specs=[vmem] * 3,
+        out_specs=(anywhere,) * 3,
+        scratch_shapes=[dma((3,))],
+        name="store_gradients",
+    )(*[pltpu.with_memory_space_constraint(x, pltpu.VMEM) for x in grads])
 
 
 def solution(mesh):

time: 43.6 us -> 37.6 us (0.86)
  the two profiles are of different devices: /device:TPU:238 before, /device:TPU:242 now
where the time goes in v3:
time: 37.6 us; the launch traced here: 37.4 us
  Pallas kernels  36.8 us (98%)
  between operations  0.64 us (2%)
    pallas_call x1, Pallas kernels, shards(): pl.pallas_call(kernel, out_shape=shapes, in_specs=[anywhere] * 6, out_spe...  36 us
    pallas_call x1, Pallas kernels, shards(): pl.pallas_call(store, out_shape=shapes, in_specs=[vmem] * 3, out_specs=(a...  0.85 us

profile of v3, /device:TPU:242, one launch (start us, length us, event | category | flops | bytes accessed | tf_op | source)
XLA Modules:
  0.0 37.4 jit_solution(889202471657186780)
XLA Ops:
  0.6 36.0 %attention_backward.1 = (bf16[256,1024]{1,0:T(8,128)(2,1)S(1)}, bf16[256,128]{1,0:T(8,128)(2,1)S(1)}, bf16[256,128]{1,0:T(8,128)(2,1)S(1)}) custom-call(s32[32]{0:T(128)} %tiles_hbm.1, s32[32]{0:T(128)} %pads_hbm.1, bf16[256,1024]{1,0:T(8,128)(2,1)} %q_hbm.1, bf16[256,128]{1,0:T(8,128)(2,1)} %k_hbm.1, bf16[256,128]{1,0:T(8,128)(2,1)} %v_hbm.1, ...), custom_call_target="tpu_custom_call" | custom-call | flops 2700000000 | bytes 2400000 | tf_op jit(solution)/shard_map/attention_backward/pallas_call | solution.py:386
  36.6 0.9 %store_gradients.1 = (bf16[256,1024]{1,0:T(8,128)(2,1)}, bf16[256,128]{1,0:T(8,128)(2,1)}, bf16[256,128]{1,0:T(8,128)(2,1)}) custom-call(bf16[256,1024]{1,0:T(8,128)(2,1)S(1)} %get-tuple-element.6.dq, bf16[256,128]{1,0:T(8,128)(2,1)S(1)} %get-tuple-element.7.dk, bf16[256,128]{1,0:T(8,128)(2,1)S(1)} %get-tuple-element.8.dv), custom_call_target="tpu_custom_call" | custom-call | tf_op jit(solution)/shard_map/store_gradients/pallas_call | solution.py:417

commit v4 on v3

--- a/solution.py
+++ b/solution.py
@@ -17,10 +17,11 @@
 
 
 BACK = (4, 3, 3, 2, 2, 1, 1)
+EARLY = (3, 4, 7, 8)
 def kernel(
     tiles_hbm, pads_hbm, q_hbm, k_hbm, v_hbm, g_hbm,
     dq_out, dk_out, dv_out,
-    tiles_ref, pads_ref, q, g, qt, gt, kw, vw, kt, e, p, m_ref, l_ref, f_ref, d_ref, sv, rv, sk, rk,
+    tiles_ref, pads_ref, q, g, qt, gt, kw, vw, kt, e, dp, p, m_ref, l_ref, f_ref, d_ref, sv, rv, sk, rk,
     local_sem, kss, krs, vss, vrs, svs, rvs, sks, rks,
 ):
     ctx, grp = lax.axis_index("ctx"), lax.axis_index("grp")
@@ -149,7 +150,7 @@
                 last[slot + 2].start()
 
     loads[0].wait()
-    launched(k_move, k_move_last, 3, 4)
+    launched(k_move, k_move_last, 4, 3)
     loads[2].wait()
 
     loads[4].wait()
@@ -226,16 +227,30 @@
                 w = w.astype(BF16)
                 p[rows_of(slot), cols_of(i, c)] = w
                 acc = acc + jnp.dot(w, two_heads(g, i, c), preferred_element_type=F32)
+                if slot in EARLY:
+                    d = dp[rows_of(slot), cols_of(i, c)] * w.astype(F32)
+                    d_ref[pl.ds(slot, 1), cols_of(i, c)] = jnp.sum(d, axis=0, keepdims=True)
             return acc
 
         return over_pairs(step, jnp.zeros((TILE, HEAD), F32))
+
+    def dprobs_raw(slot):
+        def step(c, carry):
+            value = vw[rows_of(slot)]
+            for i in tiles_of(slot):
+                dp[rows_of(slot), cols_of(i, c)] = jnp.dot(
+                    value, gt[:, cols_of(i, c)], preferred_element_type=F32
+                )
+            return carry
+
+        over_pairs(step)
 
     def dprobs(slot):
         def step(c, carry):
             value = vw[rows_of(slot)]
             for i in tiles_of(slot):
                 d = jnp.dot(value, gt[:, cols_of(i, c)], preferred_element_type=F32)
-                e[rows_of(slot), cols_of(i, c)] = d
+                dp[rows_of(slot), cols_of(i, c)] = d
                 d = d * p[rows_of(slot), cols_of(i, c)].astype(F32)
                 d_ref[pl.ds(slot, 1), cols_of(i, c)] = jnp.sum(d, axis=0, keepdims=True)
             return carry
@@ -252,7 +267,7 @@
     def key_part(slot):
         def step(c, acc):
             for i in tiles_of(slot):
-                d = e[rows_of(slot), cols_of(i, c)] - f_ref[pl.ds(0, 1), cols_of(i, c)]
+                d = dp[rows_of(slot), cols_of(i, c)] - f_ref[pl.ds(0, 1), cols_of(i, c)]
                 d = (p[rows_of(slot), cols_of(i, c)].astype(F32) * d).astype(BF16)
                 p[rows_of(slot), cols_of(i, c)] = d
                 acc = acc + jnp.dot(d, two_heads(q, i, c), preferred_element_type=F32)
@@ -289,11 +304,10 @@
             moves[slot].wait_recv()
 
     def relayed(moves):
-        for slot in (3, 4):
+        for slot, onward in ((4, (0, 2, 6)), (3, (1, 5))):
             moves[slot].wait_recv()
-            moves[slot - 2].start()
-            moves[slot + 2].start()
-        moves[0].start()
+            for dst in onward:
+                moves[dst].start()
 
     def sent(part, slot, moves, last, sbuf):
         sbuf[slot] = part.astype(BF16)
@@ -315,42 +329,44 @@
 
     loads[1].wait()
     turned(q, qt)
+    launched(v_move, v_move_last, 4, 3)
     scores(7)
     scores(8)
-    launched(v_move, v_move_last, 3, 4)
     relayed(k_move)
     loads[3].wait()
     turned(g, gt)
     for slot in (3, 4):
         scores(slot)
+    for slot in (7, 8):
+        dprobs_raw(slot)
     relayed(v_move)
-    for slot in (1, 5, 2, 6, 0):
+    for slot in (3, 4):
+        dprobs_raw(slot)
+    for slot in (2, 6, 0, 1, 5):
         arrived(k_move, slot)
         scores(slot)
     factors()
 
     v_part = {}
-    for slot in (1, 5, 2, 6, 0):
+    for slot in (0, 2, 6, 1, 5):
         sent(value_part(slot), slot, v_home, v_home_last, sv)
     for slot in (3, 4, 7, 8):
         v_part[slot] = value_part(slot)
-    for slot in (7, 8, 3, 4):
-        dprobs(slot)
-    for slot in (1, 5, 2, 6, 0):
+    for slot in (2, 6, 0, 1, 5):
         arrived(v_move, slot)
         dprobs(slot)
     deltas()
 
     k_part = {}
-    for slot in (1, 5, 2, 6, 0):
+    for slot in (0, 2, 6, 1, 5):
         sent(key_part(slot), slot, k_home, k_home_last, sk)
-    for slot in (3, 4):
+    for slot in (4, 3):
         added(v_part[slot], slot, v_home, v_home_last, sv, rv)
     for slot in (3, 4, 7, 8):
         k_part[slot] = key_part(slot)
     query_part(0, dq_out)
+    added(k_part[4], 4, k_home, k_home_last, sk, rk)
     added(k_part[3], 3, k_home, k_home_last, sk, rk)
-    added(k_part[4], 4, k_home, k_home_last, sk, rk)
     query_part(1, dq_out)
     settled(v_part, v_home, rv, dv_out)
     settled(k_part, k_home, rk, dk_out)
@@ -399,6 +415,7 @@
             pltpu.VMEM((window, HEAD), BF16),
             pltpu.VMEM((HEAD, window), BF16),
             pltpu.VMEM((window, both), F32),
+            pltpu.VMEM((window, both), F32),
             pltpu.VMEM((window, both), BF16),
             pltpu.VMEM((16, both), F32),
             pltpu.VMEM((16, both), F32),

time: 37.6 us -> 36.4 us (0.968)
  Pallas kernels: 36.8 us -> 35.6 us
    pallas_call x1, Pallas kernels: 36 us -> 34.7 us  [shards(): pl.pallas_call(kernel, out_shape=shapes, in_specs=[anywhere] * 6, out_spe...]
where the time goes in v4:
time: 36.4 us; the launch traced here: 36.2 us
  Pallas kernels  35.6 us (98%)
  between operations  0.64 us (2%)
    pallas_call x1, Pallas kernels, shards(): pl.pallas_call(kernel, out_shape=shapes, in_specs=[anywhere] * 6, out_spe...  34.7 us
    pallas_call x1, Pallas kernels, shards(): pl.pallas_call(store, out_shape=shapes, in_specs=[vmem] * 3, out_specs=(a...  0.85 us

profile of v4, /device:TPU:242, one launch (start us, length us, event | category | flops | bytes accessed | tf_op | source)
XLA Modules:
  0.0 36.2 jit_solution(1337346252142696904)
XLA Ops:
  0.6 34.7 %attention_backward.1 = (bf16[256,1024]{1,0:T(8,128)(2,1)S(1)}, bf16[256,128]{1,0:T(8,128)(2,1)S(1)}, bf16[256,128]{1,0:T(8,128)(2,1)S(1)}) custom-call(s32[32]{0:T(128)} %tiles_hbm.1, s32[32]{0:T(128)} %pads_hbm.1, bf16[256,1024]{1,0:T(8,128)(2,1)} %q_hbm.1, bf16[256,128]{1,0:T(8,128)(2,1)} %k_hbm.1, bf16[256,128]{1,0:T(8,128)(2,1)} %v_hbm.1, ...), custom_call_target="tpu_custom_call" | custom-call | flops 2700000000 | bytes 2400000 | tf_op jit(solution)/shard_map/attention_backward/pallas_call | solution.py:402
  35.4 0.9 %store_gradients.1 = (bf16[256,1024]{1,0:T(8,128)(2,1)}, bf16[256,128]{1,0:T(8,128)(2,1)}, bf16[256,128]{1,0:T(8,128)(2,1)}) custom-call(bf16[256,1024]{1,0:T(8,128)(2,1)S(1)} %get-tuple-element.6.dq, bf16[256,128]{1,0:T(8,128)(2,1)S(1)} %get-tuple-element.7.dk, bf16[256,128]{1,0:T(8,128)(2,1)S(1)} %get-tuple-element.8.dv), custom_call_target="tpu_custom_call" | custom-call | tf_op jit(solution)/shard_map/store_gradients/pallas_call | solution.py:434

commit v5 on v4

--- a/solution.py
+++ b/solution.py
@@ -329,8 +329,8 @@
 
     loads[1].wait()
     turned(q, qt)
+    scores(7)
     launched(v_move, v_move_last, 4, 3)
-    scores(7)
     scores(8)
     relayed(k_move)
     loads[3].wait()
@@ -360,11 +360,11 @@
     k_part = {}
     for slot in (0, 2, 6, 1, 5):
         sent(key_part(slot), slot, k_home, k_home_last, sk)
-    for slot in (4, 3):
-        added(v_part[slot], slot, v_home, v_home_last, sv, rv)
     for slot in (3, 4, 7, 8):
         k_part[slot] = key_part(slot)
     query_part(0, dq_out)
+    for slot in (4, 3):
+        added(v_part[slot], slot, v_home, v_home_last, sv, rv)
     added(k_part[4], 4, k_home, k_home_last, sk, rk)
     added(k_part[3], 3, k_home, k_home_last, sk, rk)
     query_part(1, dq_out)

time: 36.4 us -> 36.3 us (level)
  the two profiles are of different devices: /device:TPU:242 before, /device:TPU:16 now
where the time goes in v5:
time: 36.3 us; the launch traced here: 36.2 us
  Pallas kernels  35.5 us (98%)
  between operations  0.64 us (2%)
    pallas_call x1, Pallas kernels, shards(): pl.pallas_call(kernel, out_shape=shapes, in_specs=[anywhere] * 6, out_spe...  34.7 us
    pallas_call x1, Pallas kernels, shards(): pl.pallas_call(store, out_shape=shapes, in_specs=[vmem] * 3, out_specs=(a...  0.85 us

profile of v5, /device:TPU:16, one launch (start us, length us, event | category | flops | bytes accessed | tf_op | source)
XLA Modules:
  0.0 36.2 jit_solution(14388864587929232944)
XLA Ops:
  0.6 34.7 %attention_backward.1 = (bf16[256,1024]{1,0:T(8,128)(2,1)S(1)}, bf16[256,128]{1,0:T(8,128)(2,1)S(1)}, bf16[256,128]{1,0:T(8,128)(2,1)S(1)}) custom-call(s32[32]{0:T(128)} %tiles_hbm.1, s32[32]{0:T(128)} %pads_hbm.1, bf16[256,1024]{1,0:T(8,128)(2,1)} %q_hbm.1, bf16[256,128]{1,0:T(8,128)(2,1)} %k_hbm.1, bf16[256,128]{1,0:T(8,128)(2,1)} %v_hbm.1, ...), custom_call_target="tpu_custom_call" | custom-call | flops 2700000000 | bytes 2400000 | tf_op jit(solution)/shard_map/attention_backward/pallas_call | solution.py:402
  35.3 0.9 %store_gradients.1 = (bf16[256,1024]{1,0:T(8,128)(2,1)}, bf16[256,128]{1,0:T(8,128)(2,1)}, bf16[256,128]{1,0:T(8,128)(2,1)}) custom-call(bf16[256,1024]{1,0:T(8,128)(2,1)S(1)} %get-tuple-element.6.dq, bf16[256,128]{1,0:T(8,128)(2,1)S(1)} %get-tuple-element.7.dk, bf16[256,128]{1,0:T(8,128)(2,1)S(1)} %get-tuple-element.8.dv), custom_call_target="tpu_custom_call" | custom-call | tf_op jit(solution)/shard_map/store_gradients/pallas_call | solution.py:434
